TPU v7x, 128 devices: a whole 4x4x4 slice. The times are simulated.
128 devices in a mesh: rows: 8 (over y, x_hi), cols: 16 (over x_lo, z, core).
Axes of the slice: x: 4 (x_hi: 2, x_lo: 2; x = x_hi * 2 + x_lo), y: 4, z: 4, core: 2. Of those that a mesh axis runs over, the one named last changes fastest.
Arguments:
- incident: float32 [2, 1024, 4096], P(None, None, ('rows', 'cols')), may hold values from -6 to 6
- diag_first: float32 [4096, 4096], P('rows', 'cols'), may hold values from -1 to 2, as said below
- coupling: float32 [4096, 4096], P('rows', 'cols'), may hold values from -0.09375 to 0.09375
- diag_second: float32 [4096, 4096], P('rows', 'cols'), may hold values from -1 to 2, as said below
- trail_first: float32 [20480, 4096], P('rows', 'cols'), may hold values from -0.09375 to 0.09375
- trail_second: float32 [20480, 4096], P('rows', 'cols'), may hold values from -0.09375 to 0.09375
- trail_rhs: float32 [1024, 20480], P('cols', 'rows'), may hold values from -6 to 6
Outputs:
- solved: float32 [2, 1024, 4096], P(None, 'cols', 'rows')
- updated: float32 [1024, 20480], P('cols', 'rows')
Inputs may be any that keep to these rules, and one draw needn't show every extreme that they name: `diag_first`: lower triangular: zero above the diagonal, diagonal entries between 0.8 and 1.25. `diag_second`: lower triangular: zero above the diagonal, diagonal entries between 0.8 and 1.25.
All inputs are finite; a program needn't handle non-finite values.
Results may differ from a plain program's by a relative error of at most 0.00011.
Values sent between devices are 32-bit elements; how exact they have to be, the bound alone decides.
A program may use at most 128 MiB of HBM per device.

v0:
```python
import jax
import jax.numpy as jnp
from jax import lax
from jax.sharding import PartitionSpec as P


def product_rows(left, right):
    return lax.dot_general(
        left,
        right,
        (((1,), (1,)), ((), ())),
        precision=lax.Precision.HIGHEST,
        preferred_element_type=jnp.float32,
    )


def whole_rows(block):
    return lax.all_gather(block, "rows", axis=1, tiled=True)


def owners_apply(operand, panel_shard):
    return product_rows(operand, lax.all_gather(panel_shard, "cols", axis=1, tiled=True))


def on_device(incident, diag_first, coupling, diag_second, trail_first, trail_second, trail_rhs):
    grouped = lax.all_to_all(incident, "cols", split_axis=1, concat_axis=2, tiled=True)
    local_first = grouped[0]
    local_second = grouped[1]
    solved_first = owners_apply(whole_rows(local_first), diag_first)
    first_rows = whole_rows(solved_first)
    reduced = local_second - owners_apply(first_rows, coupling)
    solved_second = owners_apply(whole_rows(reduced), diag_second)
    second_rows = whole_rows(solved_second)
    spread_first, spread_second = (
        lax.all_to_all(first_rows, "cols", split_axis=1, concat_axis=0, tiled=True),
        lax.all_to_all(second_rows, "cols", split_axis=1, concat_axis=0, tiled=True),
    )
    eliminated = lax.psum_scatter(
        product_rows(spread_first, trail_first) + product_rows(spread_second, trail_second),
        "cols",
        scatter_dimension=0,
        tiled=True,
    )
    updated = trail_rhs - eliminated
    solved = jnp.stack([solved_first, solved_second])
    return (solved, updated)


def solution(mesh):
    placed = (
        P(None, None, ("rows", "cols")),
        P("rows", "cols"),
        P("rows", "cols"),
        P("rows", "cols"),
        P("rows", "cols"),
        P("rows", "cols"),
        P("cols", "rows"),
    )
    return jax.shard_map(
        on_device,
        mesh=mesh,
        in_specs=placed,
        out_specs=(P(None, "cols", "rows"), P("cols", "rows")),
        check_vma=False,
    )
```

profile of v0, /device:TPU:0, one launch (start us, length us, event | category | flops | bytes accessed | tf_op | source)
XLA Modules:
  0.0 527.0 jit_solution(6225580293501011959)
XLA Ops:
  7.2 2.3 copy.12
  9.5 2.3 reshape.14
  11.8 14.3 %all_to_all.53 = f32[16,1,4096]{2,1,0:T(1,128)S(1)} all-to-all(f32[16,1,4096]{2,1,0:T(1,128)S(1)} %reshape.14), channel_id=1, replica_groups=mesh['rows'=8,'cols'=16] {'cols'}, dimensions={0} | all-to-all | bytes 524288 | tf_op jit(solution)/shard_map/all_to_all | solution.py:26
  27.9 1.9 reshape.15
  29.8 1.4 copy.13
  33.5 51.5 %all-gather.8.cloned.1.call-done = f32[64,4096]{0,1:T(8,128)} async-done(((f32[64,512]{0,1:T(8,128)}), f32[64,4096]{0,1:T(8,128)}) %all-gather.8.cloned.1.call-update) | async-done | bytes 1048592 | tf_op jit(solution)/shard_map/all_gather | solution.py:18
  85.1 51.8 %all-gather.10.cloned.1.call-done = f32[512,4096]{1,0:T(8,128)} async-done(((f32[512,256]{1,0:T(8,128)}), f32[512,4096]{1,0:T(8,128)}) %all-gather.10.cloned.1.call-update) | async-done | bytes 8388624 | tf_op jit(solution)/shard_map/all_gather | solution.py:22
  136.8 13.0 %fusion.1 = f32[64,512]{1,0:T(8,128)} fusion(f32[64,4096]{0,1:T(8,128)} %all-gather.8.cloned.1.call-done, f32[512,4096]{1,0:T(8,128)} %all-gather.10.cloned.1.call-done), kind=kOutput, calls=%fused_computation.6 | convolution fusion | flops 1610612736 | bytes 9568256 | tf_op jit(solution)/shard_map/dot_general | solution.py:8
  150.8 40.9 %all-gather.14.cloned.1.call-done = f32[512,4096]{1,0:T(8,128)} async-done(((f32[512,256]{1,0:T(8,128)}), f32[512,4096]{1,0:T(8,128)}) %all-gather.14.cloned.1.call-update) | async-done | bytes 8388624 | tf_op jit(solution)/shard_map/all_gather | solution.py:22
  191.7 50.0 %all-gather.12.cloned.1.call-done = f32[64,4096]{1,0:T(8,128)} async-done(((f32[64,512]{1,0:T(8,128)}), f32[64,4096]{1,0:T(8,128)}) %all-gather.12.cloned.1.call-update) | async-done | bytes 1048592 | tf_op jit(solution)/shard_map/all_gather | solution.py:18
  241.6 12.4 %convolution_subtract_fusion = f32[64,512]{1,0:T(8,128)} fusion(f32[64,512]{1,0:T(8,128)S(1)} %copy.14, f32[64,4096]{1,0:T(8,128)} %all-gather.12.cloned.1.call-done, f32[512,4096]{1,0:T(8,128)} %all-gather.14.cloned.1.call-done), kind=kOutput, calls=%fused_computation.1 | convolution fusion | flops 1610645504 | bytes 9699328 | tf_op jit(solution)/shard_map/dot_general | solution.py:8
  254.3 39.8 %all-gather.18.cloned.1.call-done = f32[512,4096]{1,0:T(8,128)} async-done(((f32[512,256]{1,0:T(8,128)}), f32[512,4096]{1,0:T(8,128)}) %all-gather.18.cloned.1.call-update) | async-done | bytes 8388624 | tf_op jit(solution)/shard_map/all_gather | solution.py:22
  294.2 50.0 %all-gather.16.cloned.1.call-done = f32[64,4096]{1,0:T(8,128)} async-done(((f32[64,512]{1,0:T(8,128)}), f32[64,4096]{1,0:T(8,128)}) %all-gather.16.cloned.1.call-update) | async-done | bytes 1048592 | tf_op jit(solution)/shard_map/all_gather | solution.py:18
  344.2 12.4 %fusion.2 = f32[64,512]{1,0:T(8,128)} fusion(f32[64,4096]{1,0:T(8,128)} %all-gather.16.cloned.1.call-done, f32[512,4096]{1,0:T(8,128)} %all-gather.18.cloned.1.call-done), kind=kOutput, calls=%fused_computation.7 | convolution fusion | flops 1610612736 | bytes 9568256 | tf_op jit(solution)/shard_map/dot_general | solution.py:8
  356.6 2.3 copy.22
  358.9 4.6 all-to-all-start.1
  363.5 39.8 %all-gather.20.cloned.1.call-done = f32[64,4096]{1,0:T(8,128)} async-done(((f32[64,512]{1,0:T(8,128)}), f32[64,4096]{1,0:T(8,128)}) %all-gather.20.cloned.1.call-update) | async-done | bytes 1048592 | tf_op jit(solution)/shard_map/all_gather | solution.py:18
  403.3 2.4 copy.21
  405.6 4.6 all-to-all-start.2
  410.6 12.2 %fusion.3 = f32[1024,2560]{1,0:T(8,128)} fusion(f32[1024,256]{1,0:T(8,128)} %bitcast.7, f32[2560,256]{1,0:T(8,128)S(1)} %copy-done), kind=kOutput, calls=%fused_computation.8 | convolution fusion | flops 8053063680 | bytes 14155776 | tf_op jit(solution)/shard_map/dot_general | solution.py:8
  422.7 4.2 all-to-all-done.2
  426.9 14.5 %convolution_add_fusion = f32[1024,2560]{1,0:T(8,128)} fusion(f32[1024,2560]{1,0:T(8,128)} %fusion.3, f32[1024,256]{1,0:T(8,128)} %bitcast.9, f32[2560,256]{1,0:T(8,128)} %param.12), kind=kOutput, calls=%fused_computation | convolution fusion | flops 8055685120 | bytes 24641536 | tf_op jit(solution)/shard_map/dot_general | solution.py:8
  443.1 75.1 %reduce-scatter.2.cloned.1.call-done = f32[64,2560]{1,0:T(8,128)} async-done(((f32[1024,2560]{1,0:T(8,128)}), f32[64,2560]{1,0:T(8,128)}) %reduce-scatter.2.cloned.1.call-update) | async-done | bytes 655376 | tf_op jit(solution)/shard_map/reduce_scatter | solution.py:38
  518.2 2.0 sub.7
  (32 shorter events, 7.3 us)
Async XLA Ops:
  7.2 403.4 %copy-start = (f32[2560,256]{1,0:T(8,128)S(1)}, f32[2560,256]{1,0:T(8,128)}, u32[]{:S(2)}) copy-start(f32[2560,256]{1,0:T(8,128)} %param.11) | copy-start | bytes 7864324
  7.2 77.9 %all-gather.8.cloned.1.call-start = ((), (), s32[]{:S(2)}) async-start(), calls=%async_computation.4 | async-start | bytes 2359296 | tf_op jit(solution)/shard_map/all_gather | solution.py:18
  32.0 104.8 %all-gather.10.cloned.1.call-start = ((), (), s32[]{:S(2)}) async-start(), calls=%async_computation.5 | async-start | bytes 8912896 | tf_op jit(solution)/shard_map/all_gather | solution.py:22
  32.7 158.9 %all-gather.14.cloned.1.call-start = ((), (), s32[]{:S(2)}) async-start(), calls=%async_computation.7 | async-start | bytes 8912896 | tf_op jit(solution)/shard_map/all_gather | solution.py:22
  33.5 208.2 %all-gather.12.cloned.1.call-start = ((), (), s32[]{:S(2)}) async-start(), calls=%async_computation.6 | async-start | bytes 1179648 | tf_op jit(solution)/shard_map/all_gather | solution.py:18
  149.8 144.4 %all-gather.18.cloned.1.call-start = ((), (), s32[]{:S(2)}) async-start(), calls=%async_computation.9 | async-start | bytes 8912896 | tf_op jit(solution)/shard_map/all_gather | solution.py:22
  150.4 193.7 %all-gather.16.cloned.1.call-start = ((), (), s32[]{:S(2)}) async-start(), calls=%async_computation.8 | async-start | bytes 1179648 | tf_op jit(solution)/shard_map/all_gather | solution.py:18
  254.1 149.2 %all-gather.20.cloned.1.call-start = ((), (), s32[]{:S(2)}) async-start(), calls=%async_computation.10 | async-start | bytes 1179648 | tf_op jit(solution)/shard_map/all_gather | solution.py:18
  358.9 46.7 %all-to-all-start.1 = ((f32[64,16,256]{2,0,1:T(8,128)}), f32[64,16,256]{2,0,1:T(8,128)}, u32[]{:S(2)}, u32[]{:S(2)}) async-start(f32[64,16,256]{2,0,1:T(8,128)} %bitcast.36), calls=%async_computation.1 | async-start | bytes 2097152 | tf_op jit(solution)/shard_map/all_to_all | solution.py:35
  405.6 21.3 %all-to-all-start.2 = ((f32[64,16,256]{2,0,1:T(8,128)}), f32[64,16,256]{2,0,1:T(8,128)}, u32[]{:S(2)}, u32[]{:S(2)}) async-start(f32[64,16,256]{2,0,1:T(8,128)} %bitcast.35), calls=%async_computation.2 | async-start | bytes 2097152 | tf_op jit(solution)/shard_map/all_to_all | solution.py:36
  410.2 107.9 %reduce-scatter.2.cloned.1.call-start = ((), (), s32[]{:S(2)}) async-start(), calls=%async_computation.11 | async-start | bytes 11141120 | tf_op jit(solution)/shard_map/reduce_scatter | solution.py:38
  426.9 93.2 %copy-start.1 = (f32[2560,256]{1,0:T(8,128)S(1)}, f32[2560,256]{1,0:T(8,128)}, u32[]{:S(2)}) copy-start(f32[2560,256]{1,0:T(8,128)} %param.11) | copy-start | bytes 7864324
  441.4 0.9 copy-start.2
  441.4 1.0 copy-start.3
  441.4 76.8 %copy-start.4 = (f32[64,2560]{1,0:T(8,128)S(1)}, f32[64,2560]{1,0:T(8,128)}, u32[]{:S(2)}) copy-start(f32[64,2560]{1,0:T(8,128)} %param.13) | copy-start | bytes 1966084
Sparse Core Ops, SparseCore 0:
  32.1 52.8 all-gather.7
  86.7 50.0 all-gather.9
  138.5 53.1 all-gather.13
  194.4 47.1 all-gather.11
  243.1 50.9 all-gather.17
  296.9 47.1 all-gather.15
  356.7 46.5 all-gather.19
  441.6 76.5 reduce-scatter.1
where the time goes:
time: 528 us; the launch traced here: 527 us
  waiting for transfers between devices  405 us (77%)
  matrix products  64.5 us (12%)
  local copies, waits for them, and re-layouts  14.9 us (3%)
  blocking collectives  14.3 us (3%)
  between operations  14.2 us (3%)
  starting transfers between devices  10.2 us (2%)
    all_gather x4, waiting for transfers between devices, whole_rows(): return lax.all_gather(block, 'rows', axis=1, tiled=True)  191 us
    all_gather x3, waiting for transfers between devices, owners_apply(): lax.all_gather(panel_shard, 'cols', axis=1, tiled=True)  132 us
    reduce_scatter x1, waiting for transfers between devices, on_device(): lax.psum_scatter(product_rows(spread_first, trail_first) + product_rows(s...  75.1 us
    dot_general x5, matrix products, product_rows(): lax.dot_general(left, right, (((1,), (1,)), ((), ())), precision=lax.Prec...  64.5 us
    all_to_all x1, blocking collectives, on_device(): lax.all_to_all(incident, 'cols', split_axis=1, concat_axis=2, tiled=True)  14.3 us
  transfers between devices with their start and end apart: 10, of which 9 were waited for; matrix products, arithmetic and copies ran while one was open for 8% of the time, Pallas kernels for 0%

commit v1 on v0

v1 whole, which is shorter than its diff:
```python
import functools

import jax
import jax.numpy as jnp
from jax import lax
from jax.experimental import pallas as pl
from jax.experimental.pallas import tpu as pltpu
from jax.sharding import PartitionSpec as P

MESH = pl.DeviceIdType.MESH
BF = jnp.bfloat16
F32 = jnp.float32

G = 2
HG = 64 // G
HP = HG // 4
W = 512
TR = 2560
PC = 512
X_FIRST = (0, 1, 2)
Z_FIRST = (3, 4)
SEND_ORDER = (3, 0, 1, 4, 2)


def split(x):
    hi = x.astype(BF)
    return hi, (x - hi.astype(F32)).astype(BF)


def product3(left, right_hi, right_lo):
    hi, lo = split(left)

    def dot(a, b):
        return lax.dot_general(a, b, (((1,), (1,)), ((), ())), preferred_element_type=F32)

    return dot(hi, right_hi) + (dot(hi, right_lo) + dot(lo, right_hi))


def kernel(
    x_ref, d1_ref, c_ref, d2_ref, t1_ref, t2_ref, rhs_ref,
    solved_ref, updated_ref,
    own_s, sib_s, own_t, sib_t, rhs,
    wh, wl, th, tl,
    xr, xt, xs, x1b, x1s,
    part, got, summed, sol,
    upd, xa, za, zb, xb,
    loc, sib_tx, sib_rx, x_tx, x_rx, st_tx, st_rx, u_tx, u_rx,
):
    r = lax.axis_index("rows")
    c = lax.axis_index("cols")
    y, xh = r // 2, r % 2
    q, k = c // 2, c % 2
    xl, z = q // 4, q % 4
    own_lanes = pl.ds(pl.multiple_of(k * 256, 256), 256)
    sib_lanes = pl.ds(pl.multiple_of((1 - k) * 256, 256), 256)
    sibling = (r, q * 2 + (1 - k))
    diagonal = r == q

    def send(src, dst, tx, rx, dev):
        pltpu.make_async_remote_copy(
            src_ref=src, dst_ref=dst, send_sem=tx, recv_sem=rx, device_id=dev, device_id_type=MESH
        ).start()

    def settle(ref, sem):
        pltpu.make_async_copy(ref, ref, sem).wait()

    own = [(d1_ref, own_s.at[0]), (c_ref, own_s.at[1]), (d2_ref, own_s.at[2]),
           (t1_ref, own_t.at[0]), (t2_ref, own_t.at[1]), (rhs_ref, rhs)]
    loads = [pltpu.make_async_copy(src, dst, loc.at[i]) for i, (src, dst) in enumerate(own)]
    for load in loads:
        load.start()

    barrier = pltpu.get_barrier_semaphore()
    plane = [(dq, dk) for dq in range(8) for dk in range(2) if (dq, dk) != (0, 0)]

    def plane_dev(dq, dk):
        return (r, ((q + dq) % 8) * 2 + (k + dk) % 2)

    def y_dev(d):
        return (((y + d) % 4) * 2 + xh, c)

    def greet(dev):
        pl.semaphore_signal(barrier, inc=1, device_id=dev, device_id_type=MESH)

    for dq, dk in plane:
        greet(plane_dev(dq, dk))
    for d in (1, 2, 3):
        greet(y_dev(d))
    for j in range(8):
        greet((q, j * 2 + (1 - k)))

        @pl.when(jnp.logical_not(jnp.logical_and(diagonal, j == q)))
        def _():
            greet((q, j * 2 + k))

    low = lax.broadcasted_iota(jnp.int32, (32, 128), 1) < 64
    for t in range(4):
        a = x_ref[0, :, 256 * t : 256 * t + 128]
        b = x_ref[0, :, 256 * t + 128 : 256 * t + 256]
        xr[0, :, 128 * t : 128 * t + 128] = jnp.where(low, a, pltpu.roll(b, 64, 1))
        xr[1, :, 128 * t : 128 * t + 128] = jnp.where(low, pltpu.roll(a, 64, 1), b)

    pl.semaphore_wait(barrier, 33 + jnp.where(diagonal, 0, 1))

    for dk in range(2):
        kk = (k + dk) % 2
        for jy in range(4):
            rows = pl.ds(jy * 8, 8)
            for jx in range(2):
                j = jy * 2 + jx
                src, dst = xr.at[kk, rows], xt.at[c, rows]
                if dk == 1:
                    send(src, dst, x_tx.at[0], x_rx.at[0], (j, r * 2 + kk))
                else:
                    me = jnp.logical_and(diagonal, r == j)

                    @pl.when(jnp.logical_not(me))
                    def _():
                        send(src, dst, x_tx.at[0], x_rx.at[0], (j, r * 2 + kk))

                    @pl.when(me)
                    def _():
                        pltpu.make_async_copy(src, dst, x_rx.at[0]).start()

    small = [d1_ref, c_ref, d2_ref]
    send(small[0], sib_s.at[0], sib_tx.at[0], sib_rx.at[0], sibling)
    for dq, dk in plane:
        lanes = pl.ds(pl.multiple_of(((q + dq) % 8) * 128, 128), 128)
        send(x_ref.at[1, :, lanes], x1b.at[c], x_tx.at[2], x_rx.at[2], plane_dev(dq, dk))
    for i in (1, 2):
        send(small[i], sib_s.at[i], sib_tx.at[i], sib_rx.at[i], sibling)
    for i, t_ref in enumerate((t1_ref, t2_ref)):
        send(t_ref, sib_t.at[i], sib_tx.at[3 + i], sib_rx.at[3 + i], sibling)
    x1b[c] = x_ref[1, :, pl.ds(pl.multiple_of(q * 128, 128), 128)]

    def ready_small(i):
        loads[i].wait()
        wh[i, :, own_lanes], wl[i, :, own_lanes] = split(own_s[i])
        settle(sib_s.at[i], sib_rx.at[i])
        wh[i, :, sib_lanes], wl[i, :, sib_lanes] = split(sib_s[i])

    def ready_trail(i):
        loads[3 + i].wait()
        settle(sib_t.at[i], sib_rx.at[3 + i])

        @pl.loop(0, 20)
        def _(n):
            rows = pl.ds(pl.multiple_of(n * 128, 128), 128)
            th[i, rows, own_lanes], tl[i, rows, own_lanes] = split(own_t[i, rows, :])
            th[i, rows, sib_lanes], tl[i, rows, sib_lanes] = split(sib_t[i, rows, :])

    ready_small(0)
    mine = pl.ds(pl.multiple_of(y * 8, 8), 8)
    settle(xt.at[:, mine], x_rx.at[0])
    for d in (1, 2, 3):
        send(xt.at[:, mine], xt.at[:, mine], x_tx.at[1], x_rx.at[1], y_dev(d))
    ready_small(1)
    ready_small(2)
    settle(xt.at[:, pl.ds(0, 24)], x_rx.at[1])
    for n in range(4):
        block = xt[:, :, 128 * n : 128 * n + 128].reshape(512, 128)
        xs[2 * n : 2 * n + 2] = block.T.reshape(2, 64, W)

    def multiply(s, g):
        if s == 0:
            left = xs[:, g * HG : (g + 1) * HG, :]
        else:
            settle(sol.at[s - 1, g, :, pl.ds(0, 3 * HP)], st_rx.at[2, s - 1, g])
            left = sol[s - 1, g]
        out = product3(left.reshape(8 * HG, W), wh[s], wl[s])
        part[s, g] = out.reshape(8, HG, W)
        for d in range(1, 8):
            to = (q + d) % 8
            send(part.at[s, g, to], got.at[s, g, d - 1], st_tx.at[0, s, g], st_rx.at[0, s, g], (r, to * 2 + k))

    def sum_up(s, g):
        settle(got.at[s, g], st_rx.at[0, s, g])
        total = part[s, g, q]
        for d in range(7):
            total = total + got[s, g, d]
        rows = slice(g * HG, (g + 1) * HG)
        if s == 1:
            total = x1s[k, rows] - total
        else:
            solved_ref[s // 2, rows] = total
        summed[s, g] = total
        for jy in range(4):
            piece = pl.ds(jy * HP, HP)
            for jx in range(2):
                j = jy * 2 + jx
                src, dst = summed.at[s, g, piece], sol.at[s, g, q, piece]
                me = jnp.logical_and(diagonal, r == j)

                @pl.when(jnp.logical_not(me))
                def _():
                    send(src, dst, st_tx.at[1, s, g], st_rx.at[1, s, g], (j, r * 2 + k))

                @pl.when(me)
                def _():
                    pltpu.make_async_copy(src, dst, st_rx.at[1, s, g]).start()

    def spread(s, g):
        piece = pl.ds(pl.multiple_of(y * HP, HP), HP)
        settle(sol.at[s, g, :, piece], st_rx.at[1, s, g])
        for d in (1, 2, 3):
            block = sol.at[s, g, :, piece]
            send(block, block, st_tx.at[2, s, g], st_rx.at[2, s, g], y_dev(d))

    groups = range(G)
    for g in groups:
        multiply(0, g)
    ready_trail(0)
    ready_trail(1)
    for g in groups:
        sum_up(0, g)
    for g in groups:
        spread(0, g)
    settle(x1b.at[pl.ds(0, 15)], x_rx.at[2])
    x1s[...] = x1b[...].reshape(512, 128).T.reshape(2, 64, W)
    for g in groups:
        multiply(1, g)
    for g in groups:
        for p in range(5):
            columns = slice(p * PC, (p + 1) * PC)
            left = sol[0, g].reshape(8 * HG, W)
            upd[g, :, :, columns] = product3(left, th[0, columns], tl[0, columns]).reshape(8, HG, PC)
    for g in groups:
        sum_up(1, g)
    for g in groups:
        spread(1, g)
    for g in groups:
        multiply(2, g)
    for g in groups:
        sum_up(2, g)
    for g in groups:
        spread(2, g)

    across = (r, ((1 - xl) * 4 + z) * 2 + k)

    def z_dev(d):
        return (r, (xl * 4 + (z + d) % 4) * 2 + k)

    for g in groups:
        settle(sol.at[2, g, :, pl.ds(0, 3 * HP)], st_rx.at[2, 2, g])
        for p in SEND_ORDER:
            columns = slice(p * PC, (p + 1) * PC)
            left = sol[2, g].reshape(8 * HG, W)
            upd[g, :, :, columns] += product3(left, th[1, columns], tl[1, columns]).reshape(8, HG, PC)
            lanes = pl.ds(p * PC, PC)
            if p in X_FIRST:
                send(upd.at[g, pl.ds((1 - xl) * 4, 4), :, lanes], xa.at[g, p], u_tx.at[0, g, p], u_rx.at[0, g, p], across)
            else:
                for d in (1, 2, 3):
                    zz = (z + d) % 4
                    for x in range(2):
                        send(upd.at[g, x * 4 + zz, :, lanes], zb.at[g, p - 3, d - 1, x],
                             u_tx.at[0, g, p], u_rx.at[0, g, p], z_dev(d))
    for g in groups:
        for p in SEND_ORDER:
            columns = slice(p * PC, (p + 1) * PC)
            lanes = pl.ds(p * PC, PC)
            if p in X_FIRST:
                settle(xa.at[g, p], u_rx.at[0, g, p])
                upd[g, pl.ds(xl * 4, 4), :, columns] += xa[g, p]
                for d in (1, 2, 3):
                    send(upd.at[g, xl * 4 + (z + d) % 4, :, lanes], za.at[g, p, d - 1],
                         u_tx.at[1, g, p], u_rx.at[1, g, p], z_dev(d))
            else:
                settle(zb.at[g, p - 3], u_rx.at[0, g, p])
                for x in range(2):
                    terms = (zb[g, p - 3, 0, x] + zb[g, p - 3, 1, x]) + zb[g, p - 3, 2, x]
                    upd[g, x * 4 + z, :, columns] += terms
                send(upd.at[g, (1 - xl) * 4 + z, :, lanes], xb.at[g, p - 3], u_tx.at[1, g, p], u_rx.at[1, g, p], across)
    loads[5].wait()
    for g in groups:
        rows = slice(g * HG, (g + 1) * HG)
        for p in SEND_ORDER:
            columns = slice(p * PC, (p + 1) * PC)
            mine = upd[g, q, :, columns]
            if p in X_FIRST:
                settle(za.at[g, p], u_rx.at[1, g, p])
                mine = mine + ((za[g, p, 0] + za[g, p, 1]) + za[g, p, 2])
            else:
                settle(xb.at[g, p - 3], u_rx.at[1, g, p])
                mine = mine + xb[g, p - 3]
            updated_ref[rows, columns] = rhs[rows, columns] - mine

    for i in range(3):
        settle(sib_s.at[i], sib_tx.at[i])
    for i in range(2):
        settle(sib_t.at[i], sib_tx.at[3 + i])

    @pl.when(diagonal)
    def _():
        settle(xt.at[pl.ds(0, 15), pl.ds(0, 8)], x_tx.at[0])

    @pl.when(jnp.logical_not(diagonal))
    def _():
        settle(xt.at[:, pl.ds(0, 8)], x_tx.at[0])

    settle(xt.at[:, pl.ds(0, 24)], x_tx.at[1])
    settle(x1b.at[pl.ds(0, 15)], x_tx.at[2])
    for s in range(3):
        for g in groups:
            settle(got.at[s, g], st_tx.at[0, s, g])

            @pl.when(diagonal)
            def _():
                settle(sol.at[s, g, pl.ds(0, 7), pl.ds(0, HP)], st_tx.at[1, s, g])

            @pl.when(jnp.logical_not(diagonal))
            def _():
                settle(sol.at[s, g, :, pl.ds(0, HP)], st_tx.at[1, s, g])

            settle(sol.at[s, g, :, pl.ds(0, 3 * HP)], st_tx.at[2, s, g])
    for g in groups:
        for p in range(5):
            if p in X_FIRST:
                settle(xa.at[g, p], u_tx.at[0, g, p])
                settle(za.at[g, p], u_tx.at[1, g, p])
            else:
                settle(zb.at[g, p - 3], u_tx.at[0, g, p])
                settle(xb.at[g, p - 3], u_tx.at[1, g, p])


def on_device(incident, diag_first, coupling, diag_second, trail_first, trail_second, trail_rhs):
    whole = pl.BlockSpec(memory_space=pltpu.VMEM)
    far = pl.BlockSpec(memory_space=pl.ANY)
    dma = pltpu.SemaphoreType.DMA
    return pl.pallas_call(
        kernel,
        out_shape=(jax.ShapeDtypeStruct((2, 64, W), F32), jax.ShapeDtypeStruct((64, TR), F32)),
        in_specs=[whole] + [far] * 6,
        out_specs=(whole, whole),
        scratch_shapes=[
            pltpu.VMEM((3, W, 256), F32),
            pltpu.VMEM((3, W, 256), F32),
            pltpu.VMEM((2, TR, 256), F32),
            pltpu.VMEM((2, TR, 256), F32),
            pltpu.VMEM((64, TR), F32),
            pltpu.VMEM((3, W, W), BF),
            pltpu.VMEM((3, W, W), BF),
            pltpu.VMEM((2, TR, W), BF),
            pltpu.VMEM((2, TR, W), BF),
            pltpu.VMEM((2, 32, 512), F32),
            pltpu.VMEM((16, 32, 512), F32),
            pltpu.VMEM((8, 64, W), F32),
            pltpu.VMEM((16, 32, 128), F32),
            pltpu.VMEM((2, 64, W), F32),
            pltpu.VMEM((3, G, 8, HG, W), F32),
            pltpu.VMEM((3, G, 7, HG, W), F32),
            pltpu.VMEM((3, G, HG, W), F32),
            pltpu.VMEM((3, G, 8, HG, W), F32),
            pltpu.VMEM((G, 8, HG, TR), F32),
            pltpu.VMEM((G, len(X_FIRST), 4, HG, PC), F32),
            pltpu.VMEM((G, len(X_FIRST), 3, HG, PC), F32),
            pltpu.VMEM((G, len(Z_FIRST), 3, 2, HG, PC), F32),
            pltpu.VMEM((G, len(Z_FIRST), HG, PC), F32),
            dma((6,)), dma((5,)), dma((5,)), dma((3,)), dma((3,)),
            dma((3, 3, G)), dma((3, 3, G)), dma((2, G, 5)), dma((2, G, 5)),
        ],
        compiler_params=pltpu.CompilerParams(
            collective_id=0, has_side_effects=True, vmem_limit_bytes=60 * 1024 * 1024
        ),
        name="solve",
    )(jnp.swapaxes(incident, 1, 2), diag_first, coupling, diag_second, trail_first, trail_second, trail_rhs)


def solution(mesh):
    split_all = P("rows", "cols")
    return jax.shard_map(
        on_device,
        mesh=mesh,
        in_specs=(P(None, None, ("rows", "cols")),) + (split_all,) * 5 + (P("cols", "rows"),),
        out_specs=(P(None, "cols", "rows"), P("cols", "rows")),
        check_vma=False,
    )
```

time: 528 us -> 159 us (0.30)
  waiting for transfers between devices: 405 us -> 0 us
  Pallas kernels: 0 us -> 154 us
  matrix products: 64.5 us -> 0 us
  blocking collectives: 14.3 us -> 0 us
  between operations: 14.2 us -> 0.64 us
  local copies, waits for them, and re-layouts: 14.9 us -> 3.64 us
  starting transfers between devices: 10.2 us -> 0 us
    all_gather x7 -> x0, waiting for transfers between devices: 324 us -> none  [the longest x4 191 us: whole_rows(): return lax.all_gather(block, 'rows', axis=1, tiled=True)]
    pallas_call x0 -> x1, Pallas kernels: none -> 154 us  [on_device(): pl.pallas_call(kernel, out_shape=(jax.ShapeDtypeStruct((2, 64, W), F32),...]
    reduce_scatter x1 -> x0, waiting for transfers between devices: 75.1 us -> none  [on_device(): lax.psum_scatter(product_rows(spread_first, trail_first) + product_rows(s...]
    dot_general x5 -> x0, matrix products: 64.5 us -> none  [product_rows(): lax.dot_general(left, right, (((1,), (1,)), ((), ())), precision=lax.Prec...]
    all_to_all x1 -> x0, blocking collectives: 14.3 us -> none  [on_device(): lax.all_to_all(incident, 'cols', split_axis=1, concat_axis=2, tiled=True)]
    all_to_all x2 -> x0, starting transfers between devices: 9.18 us -> none  [the longest x1 4.59 us: on_device(): lax.all_to_all(first_rows, 'cols', split_axis=1, concat_axis=0, tiled=True)]
    all_to_all x4 -> x0, local copies, waits for them, and re-layouts: 6.61 us -> none  [the longest x1 2.35 us: on_device(): lax.all_to_all(second_rows, 'cols', split_axis=1, concat_axis=0, tiled=True)]
  transfers between devices with their start and end apart: 10 -> 0, of which waited for: 9 -> 0; matrix products, arithmetic and copies ran while one was open for 8% -> 0% of each run, Pallas kernels for 0% -> 0%
where the time goes in v1:
time: 159 us; the launch traced here: 158 us
  Pallas kernels  154 us (97%)
  local copies, waits for them, and re-layouts  3.64 us (2%)
    pallas_call x1, Pallas kernels, on_device(): pl.pallas_call(kernel, out_shape=(jax.ShapeDtypeStruct((2, 64, W), F32),...  154 us
    unnamed x2, local copies, waits for them, and re-layouts  3.64 us

profile of v1, /device:TPU:0, one launch (start us, length us, event | category | flops | bytes accessed | tf_op | source)
XLA Modules:
  0.0 157.9 jit_solution(18400932269773699362)
XLA Ops:
  0.6 153.6 %solve.1 = (f32[2,64,512]{2,1,0:T(8,128)}, f32[64,2560]{1,0:T(8,128)}) custom-call(f32[2,32,1024]{2,1,0:T(8,128)} %bitcast.1, f32[512,256]{1,0:T(8,128)} %d1_ref.1, f32[512,256]{1,0:T(8,128)} %c_ref.1, f32[512,256]{1,0:T(8,128)} %d2_ref.1, f32[2560,256]{1,0:T(8,128)} %t1_ref.1, f32[2560,256]{1,0:T(8,128)} %t2_ref.1, f32[64,2560]{1,0:T(8,128)} %rhs_ref.1), custom_call_target="tpu_custom_call" | custom-call | tf_op jit(solution)/shard_map/solve/pallas_call | solution.py:330
  154.2 1.7 %copy.11 = f32[2,64,512]{2,1,0:T(8,128)} copy(f32[2,64,512]{2,1,0:T(8,128)} %get-tuple-element.4) | data formatting | bytes 524288
  155.9 2.0 %copy.12 = f32[64,2560]{1,0:T(8,128)} copy(f32[64,2560]{1,0:T(8,128)} %get-tuple-element.5) | data formatting | bytes 1310720

commit v2 on v1

v2 whole, which is shorter than its diff:
```python
import functools

import jax
import jax.numpy as jnp
from jax import lax
from jax.experimental import pallas as pl
from jax.experimental.pallas import tpu as pltpu
from jax.sharding import PartitionSpec as P

MESH = pl.DeviceIdType.MESH
BF = jnp.bfloat16
F32 = jnp.float32

G = 4
HG = 64 // G
W = 512
HL = 512 // G
TR = 2560
PIECES = ((1536, 512, 0), (0, 768, 1), (768, 768, 1), (2048, 512, 0))
XW, ZW = 768, 512
STEP = 4


def split(x):
    hi = x.astype(BF)
    return hi, (x - hi.astype(F32)).astype(BF)


def product3(left, right_hi, right_lo):
    hi, lo = split(left)

    def dot(a, b):
        return lax.dot_general(a, b, (((1,), (1,)), ((), ())), preferred_element_type=F32)

    return dot(hi, right_hi) + (dot(hi, right_lo) + dot(lo, right_hi))


def kernel(
    x_ref, d1_ref, c_ref, d2_ref, t1_ref, t2_ref, rhs_ref,
    solved_ref, updated_ref,
    own_s, sib_s, own_t, sib_t, rhs,
    wh, wl, th, tl,
    xr, xt, x1b, x1s,
    part, got, summed, sol,
    upd, xa, za, zb, xb,
    loc, sib_tx, sib_rx, x_tx, x_rx, xg_tx, xg_rx, st_tx, st_rx, u_tx, u_rx,
):
    r = lax.axis_index("rows")
    c = lax.axis_index("cols")
    y, xh = r // 2, r % 2
    q, k = c // 2, c % 2
    xl, z = q // 4, q % 4
    own_lanes = pl.ds(pl.multiple_of(k * 256, 256), 256)
    sib_lanes = pl.ds(pl.multiple_of((1 - k) * 256, 256), 256)
    sibling = (r, q * 2 + (1 - k))
    diagonal = r == q

    def send(src, dst, tx, rx, dev):
        pltpu.make_async_remote_copy(
            src_ref=src, dst_ref=dst, send_sem=tx, recv_sem=rx, device_id=dev, device_id_type=MESH
        ).start()

    def settle(ref, sem):
        pltpu.make_async_copy(ref, ref, sem).wait()

    own = [(d1_ref, own_s.at[0]), (c_ref, own_s.at[1]), (d2_ref, own_s.at[2]),
           (t1_ref, own_t.at[0]), (t2_ref, own_t.at[1]), (rhs_ref, rhs)]
    loads = [pltpu.make_async_copy(src, dst, loc.at[i]) for i, (src, dst) in enumerate(own)]
    for load in loads:
        load.start()

    barrier = pltpu.get_barrier_semaphore()
    plane = [(dq, dk) for dq in range(8) for dk in range(2) if (dq, dk) != (0, 0)]

    def plane_dev(dq, dk):
        return (r, ((q + dq) % 8) * 2 + (k + dk) % 2)

    def y_dev(d):
        return (((y + d) % 4) * 2 + xh, c)

    def greet(dev):
        pl.semaphore_signal(barrier, inc=1, device_id=dev, device_id_type=MESH)

    for dq, dk in plane:
        greet(plane_dev(dq, dk))
    for d in (1, 2, 3):
        greet(y_dev(d))
    for j in range(8):
        greet((q, j * 2 + (1 - k)))

        @pl.when(jnp.logical_not(jnp.logical_and(diagonal, j == q)))
        def _():
            greet((q, j * 2 + k))

    per = 128 // HG
    place = lax.broadcasted_iota(jnp.int32, (32, 128), 1) // HG
    for core in range(2):
        for t in range(4):
            tile = None
            for j in range(per):
                chip = (t * per + j) % 8
                here = core * G + (t * per + j) // 8
                taken = x_ref[0, :, chip * 128 : chip * 128 + 128]
                shift = ((j - here) * HG) % 128
                if shift:
                    taken = pltpu.roll(taken, shift, 1)
                tile = taken if tile is None else jnp.where(place == j, taken, tile)
            xr[core, :, t * 128 : t * 128 + 128] = tile

    pl.semaphore_wait(barrier, 33 + jnp.where(diagonal, 0, 1))

    for dk in range(2):
        kk = (k + dk) % 2
        for jy in range(4):
            rows = pl.ds(jy * 8, 8)
            for jx in range(2):
                j = jy * 2 + jx
                src, dst = xr.at[kk, rows], xt.at[c, rows]
                if dk == 1:
                    send(src, dst, x_tx.at[0], x_rx.at[0], (j, r * 2 + kk))
                else:
                    me = jnp.logical_and(diagonal, r == j)

                    @pl.when(jnp.logical_not(me))
                    def _():
                        send(src, dst, x_tx.at[0], x_rx.at[0], (j, r * 2 + kk))

                    @pl.when(me)
                    def _():
                        pltpu.make_async_copy(src, dst, x_rx.at[0]).start()

    small = [d1_ref, c_ref, d2_ref]
    send(small[0], sib_s.at[0], sib_tx.at[0], sib_rx.at[0], sibling)

    def ready_small(i):
        loads[i].wait()
        wh[i, :, own_lanes], wl[i, :, own_lanes] = split(own_s[i])
        settle(sib_s.at[i], sib_rx.at[i])
        wh[i, :, sib_lanes], wl[i, :, sib_lanes] = split(sib_s[i])

    def ready_trail(i):
        loads[3 + i].wait()
        settle(sib_t.at[i], sib_rx.at[3 + i])

        @pl.loop(0, 20)
        def _(n):
            rows = pl.ds(pl.multiple_of(n * 128, 128), 128)
            th[i, rows, own_lanes], tl[i, rows, own_lanes] = split(own_t[i, rows, :])
            th[i, rows, sib_lanes], tl[i, rows, sib_lanes] = split(sib_t[i, rows, :])

    ready_small(0)
    mine = pl.ds(pl.multiple_of(y * 8, 8), 8)
    settle(xt.at[:, mine], x_rx.at[0])
    for g in range(G):
        for d in (1, 2, 3):
            block = xt.at[:, mine, pl.ds(g * HL, HL)]
            send(block, block, xg_tx.at[g], xg_rx.at[g], y_dev(d))
    send(small[1], sib_s.at[1], sib_tx.at[1], sib_rx.at[1], sibling)
    for dq, dk in plane:
        lanes = pl.ds(pl.multiple_of(((q + dq) % 8) * 128, 128), 128)
        send(x_ref.at[1, :, lanes], x1b.at[c], x_tx.at[1], x_rx.at[1], plane_dev(dq, dk))
    x1b[c] = x_ref[1, :, pl.ds(pl.multiple_of(q * 128, 128), 128)]
    send(small[2], sib_s.at[2], sib_tx.at[2], sib_rx.at[2], sibling)
    for i, t_ref in enumerate((t1_ref, t2_ref)):
        send(t_ref, sib_t.at[i], sib_tx.at[3 + i], sib_rx.at[3 + i], sibling)

    def three_lanes(s, g):
        return sol.at[s, g, :, :, pl.ds(0, 384)]

    def own_piece():
        return pl.ds(pl.multiple_of(y * 128, 128), 128)

    def multiply(s, g):
        if s == 0:
            settle(xt.at[:, pl.ds(0, 24), pl.ds(0, HL)], xg_rx.at[g])
            left = xt[:, :, g * HL : (g + 1) * HL].reshape(W, HL).T
        else:
            settle(three_lanes(s - 1, g), st_rx.at[2, s - 1, g])
            left = sol[s - 1, g].reshape(8 * HG, W)
        out = product3(left, wh[s], wl[s])
        part[s, g] = out.reshape(8, HG, W)
        for d in range(1, 8):
            to = (q + d) % 8
            send(part.at[s, g, to], got.at[s, g, d - 1], st_tx.at[0, s, g], st_rx.at[0, s, g], (r, to * 2 + k))

    def sum_up(s, g):
        settle(got.at[s, g], st_rx.at[0, s, g])
        total = part[s, g, q]
        for d in range(7):
            total = total + got[s, g, d]
        rows = slice(g * HG, (g + 1) * HG)
        if s == 1:
            total = x1s[k, rows] - total
        else:
            solved_ref[s // 2, rows] = total
        summed[s, g] = total
        for jy in range(4):
            piece = pl.ds(jy * 128, 128)
            for jx in range(2):
                j = jy * 2 + jx
                src, dst = summed.at[s, g, :, piece], sol.at[s, g, q, :, piece]
                me = jnp.logical_and(diagonal, r == j)

                @pl.when(jnp.logical_not(me))
                def _():
                    send(src, dst, st_tx.at[1, s, g], st_rx.at[1, s, g], (j, r * 2 + k))

                @pl.when(me)
                def _():
                    pltpu.make_async_copy(src, dst, st_rx.at[1, s, g]).start()

    def spread(s, g):
        block = sol.at[s, g, :, :, own_piece()]
        settle(block, st_rx.at[1, s, g])
        for d in (1, 2, 3):
            send(block, block, st_tx.at[2, s, g], st_rx.at[2, s, g], y_dev(d))

    def ready_second():
        settle(x1b.at[pl.ds(0, 15)], x_rx.at[1])
        x1s[...] = x1b[...].reshape(512, 128).T.reshape(2, 64, W)

    def first_trail(p):
        start, width, _ = PIECES[p]
        columns = slice(start, start + width)
        left = sol[0].reshape(512, W)
        upd[:, :, :, columns] = product3(left, th[0, columns], tl[0, columns]).reshape(G, 8, HG, width)

    across = (r, ((1 - xl) * 4 + z) * 2 + k)

    def z_dev(d):
        return (r, (xl * 4 + (z + d) % 4) * 2 + k)

    def second_trail(g):
        settle(three_lanes(2, g), st_rx.at[2, 2, g])
        for p, (start, width, x_first) in enumerate(PIECES):
            columns = slice(start, start + width)
            left = sol[2, g].reshape(8 * HG, W)
            upd[g, :, :, columns] += product3(left, th[1, columns], tl[1, columns]).reshape(8, HG, width)
            lanes = pl.ds(start, width)
            if x_first:
                send(upd.at[g, pl.ds((1 - xl) * 4, 4), :, lanes], xa.at[g, p - 1], u_tx.at[0, g, p], u_rx.at[0, g, p], across)
            else:
                for d in (1, 2, 3):
                    for x in range(2):
                        send(upd.at[g, x * 4 + (z + d) % 4, :, lanes], zb.at[g, p // 3, d - 1, x],
                             u_tx.at[0, g, p], u_rx.at[0, g, p], z_dev(d))

    def middle(g):
        for p, (start, width, x_first) in enumerate(PIECES):
            columns = slice(start, start + width)
            lanes = pl.ds(start, width)
            if x_first:
                settle(xa.at[g, p - 1], u_rx.at[0, g, p])
                upd[g, pl.ds(xl * 4, 4), :, columns] += xa[g, p - 1]
                for d in (1, 2, 3):
                    send(upd.at[g, xl * 4 + (z + d) % 4, :, lanes], za.at[g, p - 1, d - 1],
                         u_tx.at[1, g, p], u_rx.at[1, g, p], z_dev(d))
            else:
                n = p // 3
                settle(zb.at[g, n], u_rx.at[0, g, p])
                for x in range(2):
                    terms = (zb[g, n, 0, x] + zb[g, n, 1, x]) + zb[g, n, 2, x]
                    upd[g, x * 4 + z, :, columns] += terms
                send(upd.at[g, (1 - xl) * 4 + z, :, lanes], xb.at[g, n], u_tx.at[1, g, p], u_rx.at[1, g, p], across)

    def finish(g):
        rows = slice(g * HG, (g + 1) * HG)
        for p, (start, width, x_first) in enumerate(PIECES):
            columns = slice(start, start + width)
            total = upd[g, q, :, columns]
            if x_first:
                settle(za.at[g, p - 1], u_rx.at[1, g, p])
                total = total + ((za[g, p - 1, 0] + za[g, p - 1, 1]) + za[g, p - 1, 2])
            else:
                settle(xb.at[g, p // 3], u_rx.at[1, g, p])
                total = total + xb[g, p // 3]
            updated_ref[rows, columns] = rhs[rows, columns] - total

    order = []
    for g in range(G):
        for s in range(3):
            begin = (4 * s + g) * STEP
            order += [(begin, multiply, (s, g)), (begin + 1.5 * STEP, sum_up, (s, g)), (begin + 2.6 * STEP, spread, (s, g))]
        begin = (12 + g) * STEP
        order += [(begin, second_trail, (g,)), (12 * STEP + 9 * (g + 1), middle, (g,)), (12 * STEP + 9 * (g + 1) + 10, finish, (g,))]
    order += [(0.1, ready_small, (1,)), (0.2, ready_small, (2,)), (1.1 * STEP, ready_trail, (0,)), (2.1 * STEP, ready_second, ()),
              (3.1 * STEP, ready_trail, (1,)), (11.9 * STEP, loads[5].wait, ())]
    order += [((7.1 + 0.5 * p) * STEP, first_trail, (p,)) for p in range(4)]
    for _, work, which in sorted(order, key=lambda entry: entry[0]):
        work(*which)

    for i in range(3):
        settle(sib_s.at[i], sib_tx.at[i])
    for i in range(2):
        settle(sib_t.at[i], sib_tx.at[3 + i])

    @pl.when(diagonal)
    def _():
        settle(xt.at[pl.ds(0, 15), pl.ds(0, 8)], x_tx.at[0])

    @pl.when(jnp.logical_not(diagonal))
    def _():
        settle(xt.at[:, pl.ds(0, 8)], x_tx.at[0])

    settle(x1b.at[pl.ds(0, 15)], x_tx.at[1])
    for g in range(G):
        settle(xt.at[:, pl.ds(0, 24), pl.ds(0, HL)], xg_tx.at[g])
        for s in range(3):
            settle(got.at[s, g], st_tx.at[0, s, g])

            @pl.when(diagonal)
            def _():
                settle(sol.at[s, g, pl.ds(0, 7), :, pl.ds(0, 128)], st_tx.at[1, s, g])

            @pl.when(jnp.logical_not(diagonal))
            def _():
                settle(sol.at[s, g, :, :, pl.ds(0, 128)], st_tx.at[1, s, g])

            settle(three_lanes(s, g), st_tx.at[2, s, g])
        for p, (_, _, x_first) in enumerate(PIECES):
            if x_first:
                settle(xa.at[g, p - 1], u_tx.at[0, g, p])
                settle(za.at[g, p - 1], u_tx.at[1, g, p])
            else:
                settle(zb.at[g, p // 3], u_tx.at[0, g, p])
                settle(xb.at[g, p // 3], u_tx.at[1, g, p])


def on_device(incident, diag_first, coupling, diag_second, trail_first, trail_second, trail_rhs):
    whole = pl.BlockSpec(memory_space=pltpu.VMEM)
    far = pl.BlockSpec(memory_space=pl.ANY)
    dma = pltpu.SemaphoreType.DMA
    return pl.pallas_call(
        kernel,
        out_shape=(jax.ShapeDtypeStruct((2, 64, W), F32), jax.ShapeDtypeStruct((64, TR), F32)),
        in_specs=[whole] + [far] * 6,
        out_specs=(whole, whole),
        scratch_shapes=[
            pltpu.VMEM((3, W, 256), F32),
            pltpu.VMEM((3, W, 256), F32),
            pltpu.VMEM((2, TR, 256), F32),
            pltpu.VMEM((2, TR, 256), F32),
            pltpu.VMEM((64, TR), F32),
            pltpu.VMEM((3, W, W), BF),
            pltpu.VMEM((3, W, W), BF),
            pltpu.VMEM((2, TR, W), BF),
            pltpu.VMEM((2, TR, W), BF),
            pltpu.VMEM((2, 32, 512), F32),
            pltpu.VMEM((16, 32, 512), F32),
            pltpu.VMEM((16, 32, 128), F32),
            pltpu.VMEM((2, 64, W), F32),
            pltpu.VMEM((3, G, 8, HG, W), F32),
            pltpu.VMEM((3, G, 7, HG, W), F32),
            pltpu.VMEM((3, G, HG, W), F32),
            pltpu.VMEM((3, G, 8, HG, W), F32),
            pltpu.VMEM((G, 8, HG, TR), F32),
            pltpu.VMEM((G, 2, 4, HG, XW), F32),
            pltpu.VMEM((G, 2, 3, HG, XW), F32),
            pltpu.VMEM((G, 2, 3, 2, HG, ZW), F32),
            pltpu.VMEM((G, 2, HG, ZW), F32),
            dma((6,)), dma((5,)), dma((5,)), dma((2,)), dma((2,)), dma((G,)), dma((G,)),
            dma((3, 3, G)), dma((3, 3, G)), dma((2, G, 4)), dma((2, G, 4)),
        ],
        compiler_params=pltpu.CompilerParams(
            collective_id=0, has_side_effects=True, vmem_limit_bytes=60 * 1024 * 1024
        ),
        name="solve",
    )(jnp.swapaxes(incident, 1, 2), diag_first, coupling, diag_second, trail_first, trail_second, trail_rhs)


def solution(mesh):
    split_all = P("rows", "cols")
    return jax.shard_map(
        on_device,
        mesh=mesh,
        in_specs=(P(None, None, ("rows", "cols")),) + (split_all,) * 5 + (P("cols", "rows"),),
        out_specs=(P(None, "cols", "rows"), P("cols", "rows")),
        check_vma=False,
    )
```

time: 159 us -> 132 us (0.83)
  Pallas kernels: 154 us -> 128 us
    pallas_call x1, Pallas kernels: 154 us -> 128 us  [on_device(): pl.pallas_call(kernel, out_shape=(jax.ShapeDtypeStruct((2, 64, W), F32),...]
where the time goes in v2:
time: 132 us
  Pallas kernels  128 us (97%)
  local copies, waits for them, and re-layouts  3.64 us (3%)
    pallas_call x1, Pallas kernels, on_device(): pl.pallas_call(kernel, out_shape=(jax.ShapeDtypeStruct((2, 64, W), F32),...  128 us
    unnamed x2, local copies, waits for them, and re-layouts  3.64 us

profile of v2, /device:TPU:0, one launch (start us, length us, event | category | flops | bytes accessed | tf_op | source)
XLA Modules:
  0.0 131.8 jit_solution(8188533107055419925)
XLA Ops:
  0.6 127.5 %solve.1 = (f32[2,64,512]{2,1,0:T(8,128)}, f32[64,2560]{1,0:T(8,128)}) custom-call(f32[2,32,1024]{2,1,0:T(8,128)} %bitcast.1, f32[512,256]{1,0:T(8,128)} %d1_ref.1, f32[512,256]{1,0:T(8,128)} %c_ref.1, f32[512,256]{1,0:T(8,128)} %d2_ref.1, f32[2560,256]{1,0:T(8,128)} %t1_ref.1, f32[2560,256]{1,0:T(8,128)} %t2_ref.1, f32[64,2560]{1,0:T(8,128)} %rhs_ref.1), custom_call_target="tpu_custom_call" | custom-call | tf_op jit(solution)/shard_map/solve/pallas_call | solution.py:333
  128.2 1.7 %copy.11 = f32[2,64,512]{2,1,0:T(8,128)} copy(f32[2,64,512]{2,1,0:T(8,128)} %get-tuple-element.4) | data formatting | bytes 524288
  129.9 2.0 %copy.12 = f32[64,2560]{1,0:T(8,128)} copy(f32[64,2560]{1,0:T(8,128)} %get-tuple-element.5) | data formatting | bytes 1310720

commit v3 on v2

v3 whole, which is shorter than its diff:
```python
import functools

import jax
import jax.numpy as jnp
from jax import lax
from jax.experimental import pallas as pl
from jax.experimental.pallas import tpu as pltpu
from jax.sharding import PartitionSpec as P

MESH = pl.DeviceIdType.MESH
BF = jnp.bfloat16
F32 = jnp.float32

G = 4
HG = 64 // G
W = 512
HL = 512 // G
TR = 2560
XW, ZW = 640, 640
PIECES = ((2 * XW, ZW, 0), (0, XW, 1), (XW, XW, 1), (2 * XW + ZW, ZW, 0))
STEP = 16
SKEW = 4
STAGES = 11, 16, 24


def split(x):
    hi = x.astype(BF)
    return hi, (x - hi.astype(F32)).astype(BF)


def product3(left, right_hi, right_lo):
    hi, lo = split(left)

    def dot(a, b):
        return lax.dot_general(a, b, (((1,), (1,)), ((), ())), preferred_element_type=F32)

    return dot(hi, right_hi) + (dot(hi, right_lo) + dot(lo, right_hi))


def kernel(
    incident_ref, d1_ref, c_ref, d2_ref, t1_ref, t2_ref, rhs_ref,
    solved_out, updated_out,
    x_ref, solved_ref, updated_ref,
    own_s, sib_s, own_t, sib_t, rhs,
    wh, wl, th, tl,
    xr, xt, x1b, x1s,
    part, got, summed, sol,
    upd, xa, xrel, za, zrel, zb, xb,
    loc, sib_tx, sib_rx, x_tx, x_rx, xg_tx, xg_rx, st_tx, st_rx, u_tx, u_rx, out_sem,
):
    r = lax.axis_index("rows")
    c = lax.axis_index("cols")
    y, xh = r // 2, r % 2
    q, k = c // 2, c % 2
    xl, z = q // 4, q % 4
    own_lanes = pl.ds(pl.multiple_of(k * 256, 256), 256)
    sib_lanes = pl.ds(pl.multiple_of((1 - k) * 256, 256), 256)
    sibling = (r, q * 2 + (1 - k))
    diagonal = r == q

    def send(src, dst, tx, rx, dev):
        pltpu.make_async_remote_copy(
            src_ref=src, dst_ref=dst, send_sem=tx, recv_sem=rx, device_id=dev, device_id_type=MESH
        ).start()

    def settle(ref, sem):
        pltpu.make_async_copy(ref, ref, sem).wait()

    first = pltpu.make_async_copy(incident_ref, x_ref, loc.at[6])
    first.start()
    own = [(d1_ref, own_s.at[0]), (c_ref, own_s.at[1]), (d2_ref, own_s.at[2]),
           (t1_ref, own_t.at[0]), (t2_ref, own_t.at[1]), (rhs_ref, rhs)]
    loads = [pltpu.make_async_copy(src, dst, loc.at[i]) for i, (src, dst) in enumerate(own)]
    for load in loads:
        load.start()

    barrier = pltpu.get_barrier_semaphore()
    plane = [(dq, dk) for dq in range(8) for dk in range(2) if (dq, dk) != (0, 0)]

    def plane_dev(dq, dk):
        return (r, ((q + dq) % 8) * 2 + (k + dk) % 2)

    def y_dev(d):
        return (((y + d) % 4) * 2 + xh, c)

    def greet(dev):
        pl.semaphore_signal(barrier, inc=1, device_id=dev, device_id_type=MESH)

    for dq, dk in plane:
        greet(plane_dev(dq, dk))
    for d in (1, 2, 3):
        greet(y_dev(d))
    for j in range(8):
        greet((q, j * 2 + (1 - k)))

        @pl.when(jnp.logical_not(jnp.logical_and(diagonal, j == q)))
        def _():
            greet((q, j * 2 + k))

    first.wait()
    per = 128 // HG
    place = lax.broadcasted_iota(jnp.int32, (32, 128), 1) // HG
    for core in range(2):
        for t in range(4):
            tile = None
            for j in range(per):
                chip = (t * per + j) % 8
                here = core * G + (t * per + j) // 8
                taken = x_ref[0, :, chip * 128 : chip * 128 + 128]
                shift = ((j - here) * HG) % 128
                if shift:
                    taken = pltpu.roll(taken, shift, 1)
                tile = taken if tile is None else jnp.where(place == j, taken, tile)
            xr[core, t] = tile.reshape(4, 8, 128)

    pl.semaphore_wait(barrier, 33 + jnp.where(diagonal, 0, 1))

    for dk in range(2):
        kk = (k + dk) % 2
        for jy in range(4):
            for jx in range(2):
                j = jy * 2 + jx
                src, dst = xr.at[kk, :, jy], xt.at[:, jy, c]
                if dk == 1:
                    send(src, dst, x_tx.at[0], x_rx.at[0], (j, r * 2 + kk))
                else:
                    me = jnp.logical_and(diagonal, r == j)

                    @pl.when(jnp.logical_not(me))
                    def _():
                        send(src, dst, x_tx.at[0], x_rx.at[0], (j, r * 2 + kk))

                    @pl.when(me)
                    def _():
                        pltpu.make_async_copy(src, dst, x_rx.at[0]).start()

    small = [d1_ref, c_ref, d2_ref]
    send(small[0], sib_s.at[0], sib_tx.at[0], sib_rx.at[0], sibling)

    def ready_small(i):
        loads[i].wait()
        wh[i, :, own_lanes], wl[i, :, own_lanes] = split(own_s[i])
        settle(sib_s.at[i], sib_rx.at[i])
        wh[i, :, sib_lanes], wl[i, :, sib_lanes] = split(sib_s[i])

    def ready_trail(i):
        loads[3 + i].wait()
        settle(sib_t.at[i], sib_rx.at[3 + i])

        @pl.loop(0, 20)
        def _(n):
            rows = pl.ds(pl.multiple_of(n * 128, 128), 128)
            th[i, rows, own_lanes], tl[i, rows, own_lanes] = split(own_t[i, rows, :])
            th[i, rows, sib_lanes], tl[i, rows, sib_lanes] = split(sib_t[i, rows, :])

    ready_small(0)
    settle(xt.at[:, y], x_rx.at[0])
    for g in range(G):
        for d in (1, 2, 3):
            block = xt.at[g, y]
            send(block, block, xg_tx.at[g], xg_rx.at[g], y_dev(d))
    send(small[1], sib_s.at[1], sib_tx.at[1], sib_rx.at[1], sibling)
    for dq, dk in plane:
        lanes = pl.ds(pl.multiple_of(((q + dq) % 8) * 128, 128), 128)
        send(x_ref.at[1, :, lanes], x1b.at[c], x_tx.at[1], x_rx.at[1], plane_dev(dq, dk))
    x1b[c] = x_ref[1, :, pl.ds(pl.multiple_of(q * 128, 128), 128)]
    send(small[2], sib_s.at[2], sib_tx.at[2], sib_rx.at[2], sibling)
    for i, t_ref in enumerate((t1_ref, t2_ref)):
        send(t_ref, sib_t.at[i], sib_tx.at[3 + i], sib_rx.at[3 + i], sibling)

    def three_pieces(s, g):
        return sol.at[s, g, pl.ds(0, 3)]

    def solved_of(s, g):
        return jnp.concatenate([sol[s, g, piece].reshape(8 * HG, 128) for piece in range(4)], axis=1)

    def multiply(s, g):
        if s == 0:
            settle(xt.at[g, pl.ds(0, 3)], xg_rx.at[g])
            left = jnp.concatenate([xt[g, :, held].reshape(32, HL) for held in range(16)], axis=0).T
        else:
            settle(three_pieces(s - 1, g), st_rx.at[2, s - 1, g])
            left = solved_of(s - 1, g)
        out = product3(left, wh[s], wl[s])
        part[s, g] = out.reshape(8, HG, W)
        for d in range(1, 8):
            to = (q + d) % 8
            send(part.at[s, g, to], got.at[s, g, d - 1], st_tx.at[0, s, g], st_rx.at[0, s, g], (r, to * 2 + k))

    def sum_up(s, g):
        settle(got.at[s, g], st_rx.at[0, s, g])
        total = part[s, g, q]
        for d in range(7):
            total = total + got[s, g, d]
        rows = pl.ds(g * HG, HG)
        if s == 1:
            total = x1s[k, rows] - total
        else:
            solved_ref[s // 2, rows] = total
            pltpu.make_async_copy(solved_ref.at[s // 2, rows], solved_out.at[s // 2, rows], out_sem.at[s // 2, g]).start()
        for piece in range(4):
            summed[s, g, piece] = total[:, piece * 128 : piece * 128 + 128]
        for jy in range(4):
            for jx in range(2):
                j = jy * 2 + jx
                src, dst = summed.at[s, g, jy], sol.at[s, g, jy, q]
                me = jnp.logical_and(diagonal, r == j)

                @pl.when(jnp.logical_not(me))
                def _():
                    send(src, dst, st_tx.at[1, s, g], st_rx.at[1, s, g], (j, r * 2 + k))

                @pl.when(me)
                def _():
                    pltpu.make_async_copy(src, dst, st_rx.at[1, s, g]).start()

    def spread(s, g):
        block = sol.at[s, g, y]
        settle(block, st_rx.at[1, s, g])
        for d in (1, 2, 3):
            send(block, block, st_tx.at[2, s, g], st_rx.at[2, s, g], y_dev(d))

    def ready_second():
        settle(x1b.at[pl.ds(0, 15)], x_rx.at[1])
        x1s[...] = x1b[...].reshape(512, 128).T.reshape(2, 64, W)

    def first_trail(pair, p):
        start, width, _ = PIECES[p]
        columns = slice(start, start + width)
        both = slice(2 * pair, 2 * pair + 2)
        left = jnp.concatenate([solved_of(0, 2 * pair), solved_of(0, 2 * pair + 1)], axis=0)
        upd[both, :, :, columns] = product3(left, th[0, columns], tl[0, columns]).reshape(2, 8, HG, width)

    across = (r, ((1 - xl) * 4 + z) * 2 + k)

    def z_dev(d):
        return (r, (xl * 4 + (z + d) % 4) * 2 + k)

    ways = (1, 3)
    sides = ((z + 1) % 4, (z + 3) % 4)
    opposite = (z + 2) % 4

    def second_trail(g):
        settle(three_pieces(2, g), st_rx.at[2, 2, g])
        left = solved_of(2, g)
        for p, (start, width, x_first) in enumerate(PIECES):
            columns = slice(start, start + width)
            upd[g, :, :, columns] += product3(left, th[1, columns], tl[1, columns]).reshape(8, HG, width)
            lanes = pl.ds(start, width)
            if x_first:
                send(upd.at[g, pl.ds((1 - xl) * 4, 4), :, lanes], xa.at[g, p - 1], u_tx.at[0, g, p], u_rx.at[0, g, p], across)
            else:
                n = p // 3
                for x in range(2):
                    send(upd.at[g, x * 4 + opposite, :, lanes], zrel.at[g, n, x], u_tx.at[0, g, p], u_rx.at[0, g, p], z_dev(ways[x]))
                for x in range(2):
                    send(upd.at[g, (1 - x) * 4 + sides[x], :, lanes], zb.at[g, n, x, 1 - x],
                         u_tx.at[1, g, p], u_rx.at[1, g, p], z_dev(ways[x]))

    def middle(g):
        for p, (start, width, x_first) in enumerate(PIECES):
            columns = slice(start, start + width)
            lanes = pl.ds(start, width)
            if x_first:
                settle(xa.at[g, p - 1], u_rx.at[0, g, p])
                upd[g, pl.ds(xl * 4, 4), :, columns] += xa[g, p - 1]
                for h in range(2):
                    rows = pl.ds(h * (HG // 2), HG // 2)
                    send(upd.at[g, xl * 4 + opposite, rows, lanes], xrel.at[g, p - 1, h],
                         u_tx.at[1, g, p], u_rx.at[1, g, p], z_dev(ways[h]))
                for h in range(2):
                    rows = pl.ds((1 - h) * (HG // 2), HG // 2)
                    send(upd.at[g, xl * 4 + sides[h], rows, lanes], za.at[g, p - 1, h, rows],
                         u_tx.at[2, g, p], u_rx.at[2, g, p], z_dev(ways[h]))
            else:
                n = p // 3
                settle(zrel.at[g, n], u_rx.at[0, g, p])
                for x in range(2):
                    upd[g, x * 4 + sides[x], :, columns] += zrel[g, n, x]
                    send(upd.at[g, x * 4 + sides[x], :, lanes], zb.at[g, n, x, x], u_tx.at[1, g, p], u_rx.at[1, g, p], z_dev(ways[x]))

    def later(g):
        for p, (start, width, x_first) in enumerate(PIECES):
            columns = slice(start, start + width)
            lanes = pl.ds(start, width)
            if x_first:
                settle(xrel.at[g, p - 1], u_rx.at[1, g, p])
                for h in range(2):
                    half = slice(h * (HG // 2), (h + 1) * (HG // 2))
                    rows = pl.ds(h * (HG // 2), HG // 2)
                    upd[g, xl * 4 + sides[h], half, columns] += xrel[g, p - 1, h]
                    send(upd.at[g, xl * 4 + sides[h], rows, lanes], za.at[g, p - 1, h, rows],
                         u_tx.at[2, g, p], u_rx.at[2, g, p], z_dev(ways[h]))
            else:
                n = p // 3
                settle(zb.at[g, n], u_rx.at[1, g, p])
                for x in range(2):
                    upd[g, x * 4 + z, :, columns] += zb[g, n, 0, x] + zb[g, n, 1, x]
                send(upd.at[g, (1 - xl) * 4 + z, :, lanes], xb.at[g, n], u_tx.at[2, g, p], u_rx.at[2, g, p], across)

    def finish(g):
        rows = pl.ds(g * HG, HG)
        for p, (start, width, x_first) in enumerate(PIECES):
            columns = slice(start, start + width)
            total = upd[g, q, :, columns]
            if x_first:
                settle(za.at[g, p - 1], u_rx.at[2, g, p])
                total = total + (za[g, p - 1, 0] + za[g, p - 1, 1])
            else:
                settle(xb.at[g, p // 3], u_rx.at[2, g, p])
                total = total + xb[g, p // 3]
            updated_ref[rows, columns] = rhs[rows, columns] - total
        pltpu.make_async_copy(updated_ref.at[rows], updated_out.at[rows], out_sem.at[2, g]).start()

    order = []
    for g in range(G):
        for s in range(3):
            begin = s * STEP + g * SKEW
            order += [(begin, multiply, (s, g)), (begin + 6, sum_up, (s, g)), (begin + 10.4, spread, (s, g))]
        begin = 3 * STEP + g * SKEW
        order += [(begin, second_trail, (g,)), (begin + STAGES[0], middle, (g,)),
                  (begin + STAGES[1], later, (g,)), (begin + STAGES[2], finish, (g,))]
    order += [(0.1, ready_small, (1,)), (0.2, ready_small, (2,)), (4.4, ready_trail, (0,)), (8.4, ready_second, ()),
              (12.4, ready_trail, (1,)), (3 * STEP - 0.4, loads[5].wait, ())]
    for pair in range(2):
        order += [(STEP + (2 * pair + 1) * SKEW + 0.4 + 2 * p, first_trail, (pair, p)) for p in range(4)]
    for _, work, which in sorted(order, key=lambda entry: entry[0]):
        work(*which)

    for i in range(3):
        settle(sib_s.at[i], sib_tx.at[i])
    for i in range(2):
        settle(sib_t.at[i], sib_tx.at[3 + i])

    @pl.when(diagonal)
    def _():
        settle(xt.at[:, 0, pl.ds(0, 15)], x_tx.at[0])

    @pl.when(jnp.logical_not(diagonal))
    def _():
        settle(xt.at[:, 0], x_tx.at[0])

    settle(x1b.at[pl.ds(0, 15)], x_tx.at[1])
    for g in range(G):
        rows = pl.ds(g * HG, HG)
        settle(solved_ref.at[0, rows], out_sem.at[0, g])
        settle(solved_ref.at[1, rows], out_sem.at[1, g])
        settle(updated_ref.at[rows], out_sem.at[2, g])
        settle(xt.at[g, pl.ds(0, 3)], xg_tx.at[g])
        for s in range(3):
            settle(got.at[s, g], st_tx.at[0, s, g])

            @pl.when(diagonal)
            def _():
                settle(sol.at[s, g, 0, pl.ds(0, 7)], st_tx.at[1, s, g])

            @pl.when(jnp.logical_not(diagonal))
            def _():
                settle(sol.at[s, g, 0], st_tx.at[1, s, g])

            settle(three_pieces(s, g), st_tx.at[2, s, g])
        for p, (_, _, x_first) in enumerate(PIECES):
            if x_first:
                settle(xa.at[g, p - 1], u_tx.at[0, g, p])
                settle(xrel.at[g, p - 1], u_tx.at[1, g, p])
                settle(za.at[g, p - 1], u_tx.at[2, g, p])
            else:
                settle(zrel.at[g, p // 3], u_tx.at[0, g, p])
                settle(zb.at[g, p // 3], u_tx.at[1, g, p])
                settle(xb.at[g, p // 3], u_tx.at[2, g, p])


def hand_over(solved_in, updated_in, solved_out, updated_out, sems):
    copies = [
        pltpu.make_async_copy(solved_in, solved_out, sems.at[0]),
        pltpu.make_async_copy(updated_in, updated_out, sems.at[1]),
    ]
    for copy in copies:
        copy.start()
    for copy in copies:
        copy.wait()


def on_device(incident, diag_first, coupling, diag_second, trail_first, trail_second, trail_rhs):
    far = pl.BlockSpec(memory_space=pl.ANY)
    dma = pltpu.SemaphoreType.DMA
    shapes = (jax.ShapeDtypeStruct((2, 64, W), F32), jax.ShapeDtypeStruct((64, TR), F32))
    results = pl.pallas_call(
        kernel,
        out_shape=shapes,
        in_specs=[far] * 7,
        out_specs=(far, far),
        scratch_shapes=[
            pltpu.VMEM((2, 32, 1024), F32),
            pltpu.VMEM((2, 64, W), F32),
            pltpu.VMEM((64, TR), F32),
            pltpu.VMEM((3, W, 256), F32),
            pltpu.VMEM((3, W, 256), F32),
            pltpu.VMEM((2, TR, 256), F32),
            pltpu.VMEM((2, TR, 256), F32),
            pltpu.VMEM((64, TR), F32),
            pltpu.VMEM((3, W, W), BF),
            pltpu.VMEM((3, W, W), BF),
            pltpu.VMEM((2, TR, W), BF),
            pltpu.VMEM((2, TR, W), BF),
            pltpu.VMEM((2, G, 4, 8, HL), F32),
            pltpu.VMEM((G, 4, 16, 8, HL), F32),
            pltpu.VMEM((16, 32, 128), F32),
            pltpu.VMEM((2, 64, W), F32),
            pltpu.VMEM((3, G, 8, HG, W), F32),
            pltpu.VMEM((3, G, 7, HG, W), F32),
            pltpu.VMEM((3, G, 4, HG, 128), F32),
            pltpu.VMEM((3, G, 4, 8, HG, 128), F32),
            pltpu.VMEM((G, 8, HG, TR), F32),
            pltpu.VMEM((G, 2, 4, HG, XW), F32),
            pltpu.VMEM((G, 2, 2, HG // 2, XW), F32),
            pltpu.VMEM((G, 2, 2, HG, XW), F32),
            pltpu.VMEM((G, 2, 2, HG, ZW), F32),
            pltpu.VMEM((G, 2, 2, 2, HG, ZW), F32),
            pltpu.VMEM((G, 2, HG, ZW), F32),
            dma((7,)), dma((5,)), dma((5,)), dma((2,)), dma((2,)), dma((G,)), dma((G,)),
            dma((3, 3, G)), dma((3, 3, G)), dma((3, G, 4)), dma((3, G, 4)), dma((3, G)),
        ],
        compiler_params=pltpu.CompilerParams(
            collective_id=0, has_side_effects=True, vmem_limit_bytes=60 * 1024 * 1024
        ),
        name="solve",
    )(jnp.swapaxes(incident, 1, 2), diag_first, coupling, diag_second, trail_first, trail_second, trail_rhs)
    return pl.pallas_call(
        hand_over,
        out_shape=shapes,
        in_specs=[pl.BlockSpec(memory_space=pltpu.VMEM)] * 2,
        out_specs=(far, far),
        scratch_shapes=[dma((2,))],
        name="hand_over",
    )(*results)


def solution(mesh):
    split_all = P("rows", "cols")
    return jax.shard_map(
        on_device,
        mesh=mesh,
        in_specs=(P(None, None, ("rows", "cols")),) + (split_all,) * 5 + (P("cols", "rows"),),
        out_specs=(P(None, "cols", "rows"), P("cols", "rows")),
        check_vma=False,
    )
```

time: 132 us -> 125 us (0.947)
  Pallas kernels: 128 us -> 124 us
  local copies, waits for them, and re-layouts: 3.64 us -> 0 us
    unnamed x2 -> x0, local copies, waits for them, and re-layouts: 3.64 us -> none
    pallas_call x1 -> x2, Pallas kernels: 128 us -> 124 us  [the longest x1 122 us: on_device(): pl.pallas_call(kernel, out_shape=shapes, in_specs=[far] * 7, out_specs=(f...]
where the time goes in v3:
time: 125 us
  Pallas kernels  124 us (99%)
    pallas_call x1, Pallas kernels, on_device(): pl.pallas_call(kernel, out_shape=shapes, in_specs=[far] * 7, out_specs=(f...  122 us

profile of v3, /device:TPU:0, one launch (start us, length us, event | category | flops | bytes accessed | tf_op | source)
XLA Modules:
  0.0 125.2 jit_solution(13350299430163491480)
XLA Ops:
  0.6 122.3 %solve.1 = (f32[2,64,512]{2,1,0:T(8,128)}, f32[64,2560]{1,0:T(8,128)}) custom-call(f32[2,32,1024]{2,1,0:T(8,128)} %bitcast.1, f32[512,256]{1,0:T(8,128)} %d1_ref.1, f32[512,256]{1,0:T(8,128)} %c_ref.1, f32[512,256]{1,0:T(8,128)} %d2_ref.1, f32[2560,256]{1,0:T(8,128)} %t1_ref.1, f32[2560,256]{1,0:T(8,128)} %t2_ref.1, f32[64,2560]{1,0:T(8,128)} %rhs_ref.1), custom_call_target="tpu_custom_call" | custom-call | tf_op jit(solution)/shard_map/solve/pallas_call | solution.py:388
  122.9 2.1 %hand_over.1 = (f32[2,64,512]{2,1,0:T(8,128)}, f32[64,2560]{1,0:T(8,128)}) custom-call(f32[2,64,512]{2,1,0:T(8,128)} %get-tuple-element.4.solved_in, f32[64,2560]{1,0:T(8,128)} %get-tuple-element.5.updated_in), custom_call_target="tpu_custom_call" | custom-call | tf_op jit(solution)/shard_map/hand_over/pallas_call | solution.py:429

commit v4 on v3

--- a/solution.py
+++ b/solution.py
@@ -18,9 +18,9 @@
 TR = 2560
 XW, ZW = 640, 640
 PIECES = ((2 * XW, ZW, 0), (0, XW, 1), (XW, XW, 1), (2 * XW + ZW, ZW, 0))
-STEP = 16
+STEP = 20
 SKEW = 4
-STAGES = 11, 16, 24
+STAGES = 11, 17.5, 26.5
 
 
 def split(x):
@@ -316,7 +316,7 @@
     for g in range(G):
         for s in range(3):
             begin = s * STEP + g * SKEW
-            order += [(begin, multiply, (s, g)), (begin + 6, sum_up, (s, g)), (begin + 10.4, spread, (s, g))]
+            order += [(begin, multiply, (s, g)), (begin + 6.4, sum_up, (s, g)), (begin + 12.4, spread, (s, g))]
         begin = 3 * STEP + g * SKEW
         order += [(begin, second_trail, (g,)), (begin + STAGES[0], middle, (g,)),
                   (begin + STAGES[1], later, (g,)), (begin + STAGES[2], finish, (g,))]

time: 125 us -> 124 us (level)
    pallas_call x1, Pallas kernels: 122 us -> 121 us  [on_device(): pl.pallas_call(kernel, out_shape=shapes, in_specs=[far] * 7, out_specs=(f...]
where the time goes in v4:
time: 124 us
  Pallas kernels  123 us (99%)
    pallas_call x1, Pallas kernels, on_device(): pl.pallas_call(kernel, out_shape=shapes, in_specs=[far] * 7, out_specs=(f...  121 us

profile of v4, /device:TPU:0, one launch (start us, length us, event | category | flops | bytes accessed | tf_op | source)
XLA Modules:
  0.0 123.9 jit_solution(982231731050681182)
XLA Ops:
  0.6 121.0 %solve.1 = (f32[2,64,512]{2,1,0:T(8,128)}, f32[64,2560]{1,0:T(8,128)}) custom-call(f32[2,32,1024]{2,1,0:T(8,128)} %bitcast.1, f32[512,256]{1,0:T(8,128)} %d1_ref.1, f32[512,256]{1,0:T(8,128)} %c_ref.1, f32[512,256]{1,0:T(8,128)} %d2_ref.1, f32[2560,256]{1,0:T(8,128)} %t1_ref.1, f32[2560,256]{1,0:T(8,128)} %t2_ref.1, f32[64,2560]{1,0:T(8,128)} %rhs_ref.1), custom_call_target="tpu_custom_call" | custom-call | tf_op jit(solution)/shard_map/solve/pallas_call | solution.py:388
  121.7 2.1 %hand_over.1 = (f32[2,64,512]{2,1,0:T(8,128)}, f32[64,2560]{1,0:T(8,128)}) custom-call(f32[2,64,512]{2,1,0:T(8,128)} %get-tuple-element.4.solved_in, f32[64,2560]{1,0:T(8,128)} %get-tuple-element.5.updated_in), custom_call_target="tpu_custom_call" | custom-call | tf_op jit(solution)/shard_map/hand_over/pallas_call | solution.py:429

commit v5 on v4

--- a/solution.py
+++ b/solution.py
@@ -20,7 +20,7 @@
 PIECES = ((2 * XW, ZW, 0), (0, XW, 1), (XW, XW, 1), (2 * XW + ZW, ZW, 0))
 STEP = 20
 SKEW = 4
-STAGES = 11, 17.5, 26.5
+STAGES = 11, 17.5, 30.5
 
 
 def split(x):

time: 124 us -> 124 us (level)
  no operation moved by 1% of the time
where the time goes in v5:
time: 124 us
  Pallas kernels  123 us (99%)
    pallas_call x1, Pallas kernels, on_device(): pl.pallas_call(kernel, out_shape=shapes, in_specs=[far] * 7, out_specs=(f...  121 us

profile of v5, /device:TPU:0, one launch (start us, length us, event | category | flops | bytes accessed | tf_op | source)
XLA Modules:
  0.0 123.9 jit_solution(17392187496840547653)
XLA Ops:
  0.6 121.0 %solve.1 = (f32[2,64,512]{2,1,0:T(8,128)}, f32[64,2560]{1,0:T(8,128)}) custom-call(f32[2,32,1024]{2,1,0:T(8,128)} %bitcast.1, f32[512,256]{1,0:T(8,128)} %d1_ref.1, f32[512,256]{1,0:T(8,128)} %c_ref.1, f32[512,256]{1,0:T(8,128)} %d2_ref.1, f32[2560,256]{1,0:T(8,128)} %t1_ref.1, f32[2560,256]{1,0:T(8,128)} %t2_ref.1, f32[64,2560]{1,0:T(8,128)} %rhs_ref.1), custom_call_target="tpu_custom_call" | custom-call | tf_op jit(solution)/shard_map/solve/pallas_call | solution.py:388
  121.7 2.1 %hand_over.1 = (f32[2,64,512]{2,1,0:T(8,128)}, f32[64,2560]{1,0:T(8,128)}) custom-call(f32[2,64,512]{2,1,0:T(8,128)} %get-tuple-element.4.solved_in, f32[64,2560]{1,0:T(8,128)} %get-tuple-element.5.updated_in), custom_call_target="tpu_custom_call" | custom-call | tf_op jit(solution)/shard_map/hand_over/pallas_call | solution.py:429
